TPU v7x, 256 devices: a whole 4x4x8 slice. The times are simulated.
256 devices in a mesh: row: 16 (over z, core), col: 16 (over x, y).
Axes of the slice: x: 4, y: 4, z: 8, core: 2. Of those that a mesh axis runs over, the one named last changes fastest.
Arguments:
- start_panel: bfloat16 [262144, 128], P(('col', 'row')), may hold values from -6 to 6
- block_values: bfloat16 [16, 16, 352, 128, 128], P('row', 'col'), may hold values from -0.078125 to 0.078125
- block_rows: int32 [16, 16, 352], P('row', 'col'), may hold values from 0 to 127, as said below
- block_cols: int32 [16, 16, 352], P('row', 'col'), may hold values from 0 to 127, as said below
- block_counts: int32 [16, 16], P('row', 'col'), may hold values from 141 to 352, as said below
Outputs:
- left_panel: bfloat16 [262144, 128], P(('row', 'col'))
- right_panel: bfloat16 [262144, 128], P(('col', 'row'))
Inputs may be any that keep to these rules, and one draw needn't show every extreme that they name: `block_rows`: block rows lie in 0 to 127 within each tile; low block rows hold more blocks; in every tile some live slot names block row 127. `block_cols`: in every tile some live slot names block column 127; a position may repeat. Only the first block_counts[r, c] slots of tile (r, c) are live; some tile fills all 352 slots.
All inputs are finite; a program needn't handle non-finite values.
Results may differ from a plain program's by a relative error of at most 0.0085.
Values may be sent and summed in bfloat16 or wider, within the bound.
A program may use at most 128 MiB of HBM per device.

v0:
```python
import jax
import jax.numpy as jnp
from jax import lax
from jax.sharding import PartitionSpec as P


def tile_product(values, index_out, index_in, live_count, panel_in, out_blocks, flipped):
    block_size = values.shape[-1]
    pieces = panel_in.reshape(-1, block_size, panel_in.shape[1])
    selected = jnp.take(pieces, index_in, axis=0)
    if flipped:
        products = jnp.einsum("kij,kip->kjp", values, selected, preferred_element_type=jnp.float32)
    else:
        products = jnp.einsum("kij,kjp->kip", values, selected, preferred_element_type=jnp.float32)
    slots = jnp.arange(values.shape[0], dtype=jnp.int32)
    live = (slots < live_count).astype(jnp.float32)
    targets = jnp.arange(out_blocks, dtype=jnp.int32)
    placement = (targets[:, None] == index_out[None, :]).astype(jnp.float32) * live[None, :]
    summed = jnp.einsum("ok,kip->oip", placement, products, precision=lax.Precision.HIGHEST)
    return summed.reshape(out_blocks * block_size, panel_in.shape[1])


def gram_local(y_rounded, nodes_total):
    return jnp.dot(y_rounded.T, y_rounded, preferred_element_type=jnp.float32) / nodes_total


def apply_factor(y_rounded, gram_total):
    lower = jnp.linalg.cholesky(gram_total)
    identity = jnp.eye(gram_total.shape[0], dtype=jnp.float32)
    inverse = jax.scipy.linalg.solve_triangular(lower, identity, lower=True)
    solved = jnp.dot(y_rounded.astype(jnp.float32), inverse.T, precision=lax.Precision.HIGHEST)
    return solved.astype(jnp.bfloat16)


def global_gram(y_rounded, nodes_total):
    partial_value = gram_local(y_rounded, nodes_total)
    return lax.psum(partial_value, ("row", "col"))


def local(start_panel, block_values, block_rows, block_cols, block_counts):
    group_rows = start_panel.shape[0]
    row_devices = lax.axis_size("row")
    col_devices = lax.axis_size("col")
    nodes_total = group_rows * row_devices * col_devices
    values = block_values[0, 0]
    rows_local = block_rows[0, 0]
    cols_local = block_cols[0, 0]
    live_count = block_counts[0, 0]
    block_size = values.shape[-1]
    row_blocks = group_rows * col_devices // block_size
    col_blocks = group_rows * row_devices // block_size
    column_tile = lax.all_gather(start_panel, "row", axis=0, tiled=True)
    left_partial = tile_product(
        values, rows_local, cols_local, live_count, column_tile, row_blocks, False
    )
    left_group = lax.psum_scatter(left_partial, "col", scatter_dimension=0, tiled=True).astype(
        jnp.bfloat16
    )
    left_panel = apply_factor(left_group, global_gram(left_group, nodes_total))
    row_tile = lax.all_gather(left_panel, "col", axis=0, tiled=True)
    right_partial = tile_product(
        values, cols_local, rows_local, live_count, row_tile, col_blocks, True
    )
    right_group = lax.psum_scatter(right_partial, "row", scatter_dimension=0, tiled=True).astype(
        jnp.bfloat16
    )
    right_panel = apply_factor(right_group, global_gram(right_group, nodes_total))
    return (left_panel, right_panel)


def solution(mesh):
    return jax.shard_map(
        local,
        mesh=mesh,
        in_specs=(
            P(("col", "row"), None),
            P("row", "col", None, None, None),
            P("row", "col", None),
            P("row", "col", None),
            P("row", "col"),
        ),
        out_specs=(P(("row", "col"), None), P(("col", "row"), None)),
        check_vma=False,
    )
```

profile of v0, /device:TPU:1, one launch (start us, length us, event | category | flops | bytes accessed | tf_op | source)
XLA Modules:
  0.0 980.3 jit_solution(696161726911754510)
XLA Ops:
  7.2 0.0 all-gather.3.cloned.1.call-start
  7.2 0.7 all-gather.3.cloned.1.call-update
  7.9 0.0 reduce-scatter.3.cloned.1.call-start
  8.6 0.7 reduce.4
  9.3 0.7 reduce.5
  10.0 46.1 %all-gather.3.cloned.1.call-done = bf16[16384,128]{1,0:T(8,128)(2,1)} async-done(((bf16[1024,128]{1,0:T(8,128)(2,1)}), bf16[16384,128]{1,0:T(8,128)(2,1)}) %all-gather.3.cloned.1.call-update) | async-done | bytes 4194320 | tf_op jit(solution)/shard_map/all_gather | solution.py:52
  56.2 13.2 %gather_fusion = bf16[352,128,128]{2,1,0:T(8,128)(2,1)} fusion(bf16[128,128,128]{2,1,0:T(8,128)(2,1)} %bitcast.45, s32[1024]{0:T(1024)S(1)} %pad_clamp_fusion.1), kind=kCustom, calls=%fused_computation.clone | custom fusion | bytes 23070080 | tf_op jit(solution)/shard_map/jit(_take)/gather | solution.py:10
  69.4 21.3 %fusion.6 = f32[352,128,128]{2,1,0:T(8,128)} fusion(bf16[1,1,352,128,128]{4,3,2,1,0:T(8,128)(2,1)} %param.11, bf16[352,128,128]{2,1,0:T(8,128)(2,1)} %gather_fusion, pred[352]{0:T(512)(128)(4,1)S(1)} %compare_and_fusion.1), kind=kOutput, calls=%fused_computation.8 | convolution fusion | flops 1482162176 | bytes 46137696 | tf_op jit(solution)/shard_map/kij,kjp->kip/dot_general | solution.py:14
  90.6 23.6 %copy.17 = f32[352,128,128]{1,0,2:T(8,128)} copy(f32[352,128,128]{2,1,0:T(8,128)} %fusion.6) | data formatting | bytes 46137344 | tf_op jit(solution)/shard_map/kij,kjp->kip/dot_general | solution.py:14
  114.2 19.5 %fusion.2 = f32[128,128,128]{2,0,1:T(8,128)S(1)} fusion(f32[352,128,128]{1,0,2:T(8,128)} %copy.17, f32[352]{0:T(512)S(1)} %fusion.38, s32[352]{0:T(512)S(1)} %reduce.4), kind=kOutput, calls=%fused_computation.4 | convolution fusion | flops 8858460160 | bytes 31460096 | tf_op jit(solution)/shard_map/ok,kip->oip/dot_general | solution.py:19
  133.7 8.1 copy.11
  141.8 0.0 reduce-scatter.3.cloned.1.call-update
  141.8 0.0 all-reduce.3.cloned.1.call-start
  141.9 87.0 %reduce-scatter.3.cloned.1.call-done = f32[1024,128]{1,0:T(8,128)} async-done(((f32[16384,128]{1,0:T(8,128)}), f32[1024,128]{1,0:T(8,128)}) %reduce-scatter.3.cloned.1.call-update) | async-done | bytes 524304 | tf_op jit(solution)/shard_map/reduce_scatter | solution.py:56
  228.9 2.1 convolution_multiply_fusion.1
  231.0 0.0 all-reduce.3.cloned.1.call-update
  231.0 0.0 all-gather.5.cloned.1.call-start
  231.1 242.5 %all-reduce.3.cloned.1.call-done = f32[128,128]{0,1:T(8,128)} async-done(((f32[128,128]{0,1:T(8,128)}), f32[128,128]{0,1:T(8,128)}) %all-reduce.3.cloned.1.call-update) | async-done | bytes 65552 | tf_op jit(solution)/shard_map/psum | solution.py:37
  473.6 0.9 copy.13
  474.6 0.9 fusion.37
  475.4 11.7 %cholesky.44 = f32[128,128]{1,0:T(8,128)S(1)} custom-call(f32[128,128]{1,0:T(8,128)S(1)} %fusion.37), custom_call_target="Cholesky" | custom-call | tf_op jit(solution)/shard_map/jit(cholesky)/cholesky | solution.py:28
  487.2 0.6 compare_reduce_fusion.1
  487.8 0.7 fusion.32
  488.5 9.8 %custom-call.6 = f32[1,128,128]{1,2,0:T(8,128)S(1)} custom-call(f32[1,128,128]{2,1,0:T(8,128)S(1)} %fusion.32), custom_call_target="InvertDiagBlocksLowerTriangular" | custom-call | tf_op jit(solution)/shard_map/jit(_solve_triangular)/triangular_solve | solution.py:30
  498.3 0.3 fusion.24
  498.6 2.1 convolution_convert_fusion.1
  500.7 0.0 all-gather.5.cloned.1.call-update
  500.7 0.3 reduce-scatter.5.cloned.1.call-start
  501.0 52.5 %all-gather.5.cloned.1.call-done = bf16[16384,128]{1,0:T(8,128)(2,1)} async-done(((bf16[1024,128]{1,0:T(8,128)(2,1)}), bf16[16384,128]{1,0:T(8,128)(2,1)}) %all-gather.5.cloned.1.call-update) | async-done | bytes 4194320 | tf_op jit(solution)/shard_map/all_gather | solution.py:60
  553.5 13.2 %gather_fusion.1 = bf16[352,128,128]{2,1,0:T(8,128)(2,1)} fusion(bf16[128,128,128]{2,1,0:T(8,128)(2,1)} %bitcast.46, s32[1024]{0:T(1024)S(1)} %pad_clamp_fusion), kind=kCustom, calls=%fused_computation.1.clone | custom fusion | bytes 23070080 | tf_op jit(solution)/shard_map/jit(_take)/gather | solution.py:10
  566.7 14.6 %fusion.4 = f32[352,128,128]{2,1,0:T(8,128)} fusion(bf16[1,1,352,128,128]{4,3,2,1,0:T(8,128)(2,1)} %param.11, bf16[352,128,128]{2,1,0:T(8,128)(2,1)} %gather_fusion.1, pred[352]{0:T(512)(128)(4,1)S(1)} %compare_and_fusion), kind=kOutput, calls=%fused_computation.6 | convolution fusion | flops 1482162176 | bytes 46137696 | tf_op jit(solution)/shard_map/kij,kip->kjp/dot_general | solution.py:12
  581.3 23.6 %copy.19 = f32[352,128,128]{1,0,2:T(8,128)} copy(f32[352,128,128]{2,1,0:T(8,128)} %fusion.4) | data formatting | bytes 46137344 | tf_op jit(solution)/shard_map/kij,kip->kjp/dot_general | solution.py:12
  604.8 19.6 %fusion = f32[128,128,128]{2,0,1:T(8,128)S(1)} fusion(f32[352,128,128]{1,0,2:T(8,128)} %copy.19, s32[352]{0:T(512)S(1)} %reduce.5, f32[352]{0:T(512)S(1)} %fusion.38), kind=kOutput, calls=%fused_computation.2 | convolution fusion | flops 8858460160 | bytes 31460096 | tf_op jit(solution)/shard_map/ok,kip->oip/dot_general | solution.py:19
  624.5 8.1 copy.14
  632.5 0.0 reduce-scatter.5.cloned.1.call-update
  632.6 0.0 all-reduce.5.cloned.1.call-start
  632.6 67.5 %reduce-scatter.5.cloned.1.call-done = f32[1024,128]{1,0:T(8,128)} async-done(((f32[16384,128]{1,0:T(8,128)}), f32[1024,128]{1,0:T(8,128)}) %reduce-scatter.5.cloned.1.call-update) | async-done | bytes 524304 | tf_op jit(solution)/shard_map/reduce_scatter | solution.py:64
  700.1 2.1 convolution_multiply_fusion
  702.2 0.0 all-reduce.5.cloned.1.call-update
  702.3 243.6 %all-reduce.5.cloned.1.call-done = f32[128,128]{0,1:T(8,128)} async-done(((f32[128,128]{0,1:T(8,128)}), f32[128,128]{0,1:T(8,128)}) %all-reduce.5.cloned.1.call-update) | async-done | bytes 65552 | tf_op jit(solution)/shard_map/psum | solution.py:37
  945.9 0.9 copy.16
  946.9 0.9 fusion.35
  947.7 11.7 %cholesky.55 = f32[128,128]{1,0:T(8,128)S(1)} custom-call(f32[128,128]{1,0:T(8,128)S(1)} %fusion.35), custom_call_target="Cholesky" | custom-call | tf_op jit(solution)/shard_map/jit(cholesky)/cholesky | solution.py:28
  959.5 0.6 compare_reduce_fusion
  960.1 0.7 fusion.33
  960.8 9.8 %custom-call.7 = f32[1,128,128]{1,2,0:T(8,128)S(1)} custom-call(f32[1,128,128]{2,1,0:T(8,128)S(1)} %fusion.33), custom_call_target="InvertDiagBlocksLowerTriangular" | custom-call | tf_op jit(solution)/shard_map/jit(_solve_triangular)/triangular_solve | solution.py:30
  970.6 0.3 fusion.22
  970.9 2.1 convolution_convert_fusion
  (9 shorter events, 0.1 us)
Async XLA Ops:
  7.2 49.0 %all-gather.3.cloned.1.call-start = ((), (), s32[]{:S(2)}) async-start(), calls=%async_computation.2 | async-start | bytes 4456448 | tf_op jit(solution)/shard_map/all_gather | solution.py:52
  7.9 221.0 %reduce-scatter.3.cloned.1.call-start = ((), (), s32[]{:S(2)}) async-start(), calls=%async_computation.3 | async-start | bytes 8912896 | tf_op jit(solution)/shard_map/reduce_scatter | solution.py:56
  141.8 331.8 %all-reduce.3.cloned.1.call-start = ((), (), s32[]{:S(2)}) async-start(), calls=%async_computation.4 | async-start | bytes 131072 | tf_op jit(solution)/shard_map/psum | solution.py:37
  231.0 322.5 %all-gather.5.cloned.1.call-start = ((), (), s32[]{:S(2)}) async-start(), calls=%async_computation.5 | async-start | bytes 4456448 | tf_op jit(solution)/shard_map/all_gather | solution.py:60
  500.7 199.4 %reduce-scatter.5.cloned.1.call-start = ((), (), s32[]{:S(2)}) async-start(), calls=%async_computation.6 | async-start | bytes 8912896 | tf_op jit(solution)/shard_map/reduce_scatter | solution.py:64
  632.6 313.4 %all-reduce.5.cloned.1.call-start = ((), (), s32[]{:S(2)}) async-start(), calls=%async_computation.7 | async-start | bytes 131072 | tf_op jit(solution)/shard_map/psum | solution.py:37
Sparse Core Ops, SparseCore 0:
  9.8 46.3 all-gather.2
  142.0 86.9 reduce-scatter.2
  235.0 238.5 all-reduce.2
  500.8 52.6 all-gather.4
  632.7 67.4 reduce-scatter.4
  706.1 239.7 all-reduce.4
where the time goes:
time: 989 us; the launch traced here: 980 us
  waiting for transfers between devices  740 us (75%)
  local copies, waits for them, and re-layouts  91.5 us (9%)
  matrix products  84 us (8%)
  other arithmetic  48.9 us (5%)
  between operations  15.3 us (2%)
    psum x2, waiting for transfers between devices, global_gram(): return lax.psum(partial_value, ('row', 'col'))  486 us
    reduce_scatter x1, waiting for transfers between devices, local(): lax.psum_scatter(left_partial, 'col', scatter_dimension=0, tiled=True)  87 us
    reduce_scatter x1, waiting for transfers between devices, local(): lax.psum_scatter(right_partial, 'row', scatter_dimension=0, tiled=True)  67.5 us
    all_gather x1, waiting for transfers between devices, local(): row_tile = lax.all_gather(left_panel, 'col', axis=0, tiled=True)  52.5 us
    all_gather x1, waiting for transfers between devices, local(): column_tile = lax.all_gather(start_panel, 'row', axis=0, tiled=True)  46.1 us
    dot_general x2, matrix products, tile_product(): jnp.einsum('ok,kip->oip', placement, products, precision=lax.Precision.HI...  39.1 us
    gather x2, local copies, waits for them, and re-layouts, tile_product(): selected = jnp.take(pieces, index_in, axis=0)  26.3 us
    another operation x6, other arithmetic, apply_factor(): lower = jnp.linalg.cholesky(gram_total)  24.8 us
  transfers between devices with their start and end apart: 6, of which 6 were waited for; matrix products, arithmetic and copies ran while one was open for 0% of the time, Pallas kernels for 0%

commit v1 on v0

v1 whole, which is shorter than its diff:
```python
import functools

import jax
import jax.numpy as jnp
from jax import lax
from jax.experimental import pallas as pl
from jax.experimental.pallas import tpu as pltpu
from jax.sharding import PartitionSpec as P

MESH = pl.DeviceIdType.MESH
F32 = jnp.float32
BF16 = jnp.bfloat16
HIGHEST = lax.Precision.HIGHEST

H = 2
PH = 64
NZ = 8
UNROLL = 16
SENDS = 320


class Copies:
    def __init__(self, send_sems, recv_sems):
        self.send_sems, self.recv_sems = send_sems, recv_sems
        self.index, self.sent = {}, []

    def sems(self, name):
        number = self.index.setdefault(name, len(self.index))
        assert number < SENDS
        return self.send_sems.at[number], self.recv_sems.at[number]

    def make(self, name, src, dst, device):
        send, recv = self.sems(name)
        return pltpu.make_async_remote_copy(
            src_ref=src, dst_ref=dst, send_sem=send, recv_sem=recv, device_id=device, device_id_type=MESH
        )

    def send(self, name, src, dst, device):
        copy = self.make(name, src, dst, device)
        copy.start()
        self.sent.append(copy)

    def arrived(self, name, dst, device):
        self.make(name, dst, dst, device).wait_recv()

    def drain(self):
        for copy in self.sent:
            copy.wait_send()
        self.sent = []


def factor_inverse(gram_ref, work, inv):
    n = gram_ref.shape[0]
    lanes = lax.broadcasted_iota(jnp.int32, (8, n), 1)
    subs = lax.broadcasted_iota(jnp.int32, (8, n), 0)
    work[...] = gram_ref[...]
    rows = lax.broadcasted_iota(jnp.int32, (n, n), 0)
    cols = lax.broadcasted_iota(jnp.int32, (n, n), 1)
    inv[...] = jnp.where(rows == cols, 1.0, 0.0).astype(F32)

    def block(jb, carry):
        start = pl.multiple_of(jb * 8, 8)
        d = pltpu.roll(work[pl.ds(start, 8), :], lax.rem(n - start, n), 1)
        m = inv[pl.ds(start, 8), :]
        scale = jnp.zeros((8, n), F32)
        for i in range(8):
            pivot = jnp.broadcast_to(d[i : i + 1, i : i + 1], (8, n))
            column = jnp.broadcast_to(d[:, i : i + 1], (8, n))
            factor = jnp.where(subs > i, column / pivot, 0.0)
            scale = jnp.where(subs == i, pivot, scale)
            d = d - factor * d[i : i + 1, :]
            m = m - factor * m[i : i + 1, :]
        d = pltpu.roll(d, start, 1)
        multipliers = jnp.where(lanes >= start + 8, d / scale, 0.0)
        work[...] = work[...] - lax.dot_general(
            multipliers, d, (((0,), (0,)), ((), ())), precision=HIGHEST, preferred_element_type=F32
        )
        inv[...] = inv[...] - lax.dot_general(
            multipliers, m, (((0,), (0,)), ((), ())), precision=HIGHEST, preferred_element_type=F32
        )
        inv[pl.ds(start, 8), :] = m / jnp.sqrt(scale)
        return carry

    lax.fori_loop(0, n // 8, block, 0)


def kernel(
    nodes_total,
    codes,
    keeps,
    lasts,
    start_ref,
    values_hbm,
    left_out,
    right_out,
    values,
    gathered,
    sums,
    partial,
    partial2,
    relay1,
    full1,
    mid,
    mid_own,
    relay2,
    full2,
    left_all,
    left_y,
    pair_in,
    ring_out,
    ring_in,
    z_sum,
    right_y,
    gram_part,
    gram_in1,
    gram_slice,
    gram_in2,
    gram_total,
    work,
    inv1,
    inv2,
    local_sem,
    send_sems,
    recv_sems,
):
    slots = values_hbm.shape[0]
    r = lax.axis_index("row")
    c = lax.axis_index("col")
    z, core = r // 2, lax.rem(r, 2)
    position = {"x": c // 4, "y": lax.rem(c, 4)}
    x, y = position["x"], position["y"]
    sibling = {"row": 2 * z + 1 - core}
    z_next = ({"row": lax.rem(r + 2, 16)}, {"row": lax.rem(r + 14, 16)})
    nearby = {
        "x": ({"col": lax.rem(c + 4, 16)}, {"col": lax.rem(c + 12, 16)}),
        "y": ({"col": 4 * x + lax.rem(y + 1, 4)}, {"col": 4 * x + lax.rem(y + 3, 4)}),
    }
    axes = (("x", "y"), ("y", "x"))
    copies = Copies(send_sems, recv_sems)
    chunks = [(h, path) for h in range(H) for path in range(2)]

    load_values = pltpu.make_async_copy(values_hbm, values, local_sem)
    load_values.start()

    barrier = pltpu.get_barrier_semaphore()
    for t in range(1, 16):
        pl.semaphore_signal(barrier, inc=1, device_id={"row": lax.rem(r + t, 16)}, device_id_type=MESH)
        pl.semaphore_signal(barrier, inc=1, device_id={"col": lax.rem(c + t, 16)}, device_id_type=MESH)

    for b in range(8):
        turned = start_ref[128 * b : 128 * b + 128, :].astype(F32).T.astype(BF16)
        for h in range(H):
            gathered[h, r * 8 + b] = turned[PH * h : PH * h + PH, :]
    sums[slots] = jnp.zeros((128, 128), BF16)
    pl.semaphore_wait(barrier, 30)

    def group(h, number, first=0, count=8):
        return gathered.at[h, pl.ds(number * 8 + first, count)]

    for h in range(H):
        own = group(h, r)
        for way in range(2):
            copies.send(("gz", h, way, 1), own, own, z_next[way])
    for h in range(H):
        own = group(h, r)
        copies.send(("gs", h, 0, 0), own, own, sibling)

    def origin(way, s):
        return lax.rem(r + (32 - 2 * s if way == 0 else 2 * s), 16)

    def origin_sibling(way, s):
        return lax.rem(2 * z + 1 - core + (32 - 2 * s if way == 0 else 2 * s), 16)

    for s in range(1, 5):
        for h in range(H):
            for way in range(2):
                piece = group(h, origin(way, s)) if s < 4 else group(h, origin(way, s), 4 * way, 4)
                copies.arrived(("gz", h, way, s), piece, z_next[way])
                if s < 3:
                    copies.send(("gz", h, way, s + 1), piece, piece, z_next[way])
                elif s == 3:
                    half = group(h, origin(way, s), 4 * way, 4)
                    copies.send(("gz", h, way, 4), half, half, z_next[way])
                copies.send(("gs", h, way, s), piece, piece, sibling)
    for h in range(H):
        copies.arrived(("gs", h, 0, 0), group(h, 2 * z + 1 - core), sibling)
        for s in range(1, 5):
            for way in range(2):
                number = origin_sibling(way, s)
                piece = group(h, number) if s < 4 else group(h, number, 4 * way, 4)
                copies.arrived(("gs", h, way, s), piece, sibling)
    load_values.wait()

    def product(side, panel, out):
        contract = (((1,), (1,)), ((), ())) if side == 0 else (((1,), (0,)), ((), ()))

        def some_slots(step, total):
            for u in range(UNROLL):
                k = step * UNROLL + u
                code = codes[side * slots + k]
                block = values[code & 511]
                piece = panel[:, code >> 9].reshape(128, 128)
                term = lax.dot_general(piece, block, contract, preferred_element_type=F32)
                total = total * keeps[side * slots + k] + term
                sums[k] = total.astype(BF16)
            return total

        lax.fori_loop(0, slots // UNROLL, some_slots, jnp.zeros((128, 128), F32))

        def some_blocks(step, carry):
            for u in range(8):
                q = step * 8 + u
                out[:, q] = sums[lasts[side * 128 + q]].reshape(H, PH, 128)
            return carry

        lax.fori_loop(0, 16, some_blocks, 0)

    product(0, gathered, partial)

    def slab(h, path, d1, first=0, count=4):
        return (h, pl.ds(path * 64 + d1 * 16 + first * 4, count * 4))

    for h, path in chunks:
        axis = axes[path][0]
        m = position[axis]
        for way in range(2):
            far = lax.rem(m + 2, 4)
            near = lax.rem(m + (1 if way == 0 else 3), 4)
            src = partial.at[slab(h, path, far, 2 * way, 2)]
            copies.send(("r1", h, path, way, 0), src, relay1.at[h, path, way], nearby[axis][way])
            src = partial.at[slab(h, path, near, 2 - 2 * way, 2)]
            dst = full1.at[h, path, way, pl.ds(8 - 8 * way, 8)]
            copies.send(("r1", h, path, way, 1), src, dst, nearby[axis][way])
    for h, path in chunks:
        axis = axes[path][0]
        m = position[axis]
        for way in range(2):
            near = lax.rem(m + (1 if way == 0 else 3), 4)
            copies.arrived(("r1", h, path, way, 0), relay1.at[h, path, way], nearby[axis][way])
            where = slab(h, path, near, 2 * way, 2)
            partial[where] = (partial[where].astype(F32) + relay1[h, path, way].astype(F32)).astype(BF16)
            dst = full1.at[h, path, way, pl.ds(8 * way, 8)]
            copies.send(("r1", h, path, way, 2), partial.at[where], dst, nearby[axis][way])
    for h, path in chunks:
        axis, other = axes[path]
        m, m2 = position[axis], position[other]
        for way in range(2):
            copies.arrived(
                ("r1", h, path, way, 1), full1.at[h, path, way, pl.ds(8 - 8 * way, 8)], nearby[axis][way]
            )
            copies.arrived(("r1", h, path, way, 2), full1.at[h, path, way, pl.ds(8 * way, 8)], nearby[axis][way])
        for d2 in range(4):
            total = partial[slab(h, path, m, d2, 1)].astype(F32)
            for way in range(2):
                total = total + full1[h, path, way, 4 * d2 : 4 * d2 + 4].astype(F32)
            mid_own[h, path, d2] = total
            mid[h, path, d2] = total.astype(BF16)
        for way in range(2):
            far = lax.rem(m2 + 2, 4)
            near = lax.rem(m2 + (1 if way == 0 else 3), 4)
            src = mid.at[h, path, far, pl.ds(2 * way, 2)]
            copies.send(("r2", h, path, way, 0), src, relay2.at[h, path, way], nearby[other][way])
            src = mid.at[h, path, near, pl.ds(2 - 2 * way, 2)]
            dst = full2.at[h, path, way, pl.ds(2 - 2 * way, 2)]
            copies.send(("r2", h, path, way, 1), src, dst, nearby[other][way])
    for h, path in chunks:
        other = axes[path][1]
        m2 = position[other]
        for way in range(2):
            near = lax.rem(m2 + (1 if way == 0 else 3), 4)
            copies.arrived(("r2", h, path, way, 0), relay2.at[h, path, way], nearby[other][way])
            where = (h, path, near, pl.ds(2 * way, 2))
            mid[where] = (mid_own[where] + relay2[h, path, way].astype(F32)).astype(BF16)
            dst = full2.at[h, path, way, pl.ds(2 * way, 2)]
            copies.send(("r2", h, path, way, 2), mid.at[where], dst, nearby[other][way])

    def piece(h, path, d1, d2, first=0, count=4):
        return left_all.at[h, pl.ds(path * 64 + d1 * 16 + d2 * 4 + first, count)]

    for h, path in chunks:
        axis, other = axes[path]
        m1, m2 = position[axis], position[other]
        for way in range(2):
            copies.arrived(("r2", h, path, way, 1), full2.at[h, path, way, pl.ds(2 - 2 * way, 2)], nearby[other][way])
            copies.arrived(("r2", h, path, way, 2), full2.at[h, path, way, pl.ds(2 * way, 2)], nearby[other][way])
        total = mid_own[h, path, m2]
        for way in range(2):
            total = total + full2[h, path, way].astype(F32)
        rounded = total.astype(BF16)
        left_all[h, pl.ds(path * 64 + m1 * 16 + m2 * 4, 4)] = rounded
        for b in range(4):
            left_y[path * 4 + b, PH * h : PH * h + PH, :] = rounded[b]
        own = piece(h, path, m1, m2)
        for way in range(2):
            copies.send(("a2", h, path, 0, way, 0), own, own, nearby[axis][way])
        for way in range(2):
            copies.send(("a1", h, path, way, 0), own, own, nearby[other][way])

    def gram_begin(tag, blocks):
        total = jnp.zeros((128, 128), F32)
        for b in range(8):
            part = blocks[b]
            total = total + lax.dot_general(part, part, (((1,), (1,)), ((), ())), preferred_element_type=F32)
        gram_part[tag] = total * (1.0 / nodes_total)
        gram_in1[tag, r] = gram_part[tag, pl.ds(pl.multiple_of(r * 8, 8), 8), :]
        for t in range(1, 16):
            to = lax.rem(r + t, 16)
            src = gram_part.at[tag, pl.ds(pl.multiple_of(to * 8, 8), 8), :]
            copies.send(("m1", tag, t), src, gram_in1.at[tag, r], {"row": to})

    def gram_middle(tag):
        for t in range(1, 16):
            copies.arrived(("m1", tag, t), gram_in1.at[tag, lax.rem(r + 16 - t, 16)], {"row": lax.rem(r + t, 16)})
        gram_slice[tag] = jnp.sum(gram_in1[tag], axis=0)
        gram_in2[tag, c] = gram_slice[tag]
        for t in range(1, 16):
            copies.send(("m2", tag, t), gram_slice.at[tag], gram_in2.at[tag, c], {"col": lax.rem(c + t, 16)})

    def gram_last(tag):
        for t in range(1, 16):
            copies.arrived(("m2", tag, t), gram_in2.at[tag, lax.rem(c + 16 - t, 16)], {"col": lax.rem(c + t, 16)})
        mine = gram_total.at[tag, pl.ds(pl.multiple_of(r * 8, 8), 8), :]
        mine[...] = jnp.sum(gram_in2[tag], axis=0)
        for t in range(1, 16):
            copies.send(("m3", tag, t), mine, mine, {"row": lax.rem(r + t, 16)})

    def gram_end(tag):
        for t in range(1, 16):
            rows = pl.ds(pl.multiple_of(lax.rem(r + 16 - t, 16) * 8, 8), 8)
            copies.arrived(("m3", tag, t), gram_total.at[tag, rows, :], {"row": lax.rem(r + t, 16)})

    gram_begin(0, left_y)
    for h, path in chunks:
        axis, other = axes[path]
        m1, m2 = position[axis], position[other]
        for way in range(2):
            d2 = lax.rem(m2 + (3 if way == 0 else 1), 4)
            copies.arrived(("a1", h, path, way, 0), piece(h, path, m1, d2), nearby[other][way])
            half = piece(h, path, m1, d2, 2 * way, 2)
            copies.send(("a1", h, path, way, 1), half, half, nearby[other][way])
            whole = piece(h, path, m1, d2)
            for way2 in range(2):
                copies.send(("a2", h, path, 1 + way, way2, 0), whole, whole, nearby[axis][way2])
    gram_middle(0)
    for h, path in chunks:
        axis, other = axes[path]
        m1, m2 = position[axis], position[other]
        far = lax.rem(m2 + 2, 4)
        for way in range(2):
            copies.arrived(("a1", h, path, way, 1), piece(h, path, m1, far, 2 * way, 2), nearby[other][way])
        whole = piece(h, path, m1, far)
        for way2 in range(2):
            copies.send(("a2", h, path, 3, way2, 0), whole, whole, nearby[axis][way2])
    gram_last(0)

    def second(m2, which):
        return lax.rem(m2 + (0, 3, 1, 2)[which], 4)

    for which in range(4):
        for h, path in chunks:
            axis, other = axes[path]
            m1, m2 = position[axis], position[other]
            d2 = second(m2, which)
            for way in range(2):
                d1 = lax.rem(m1 + (3 if way == 0 else 1), 4)
                copies.arrived(("a2", h, path, which, way, 0), piece(h, path, d1, d2), nearby[axis][way])
                half = piece(h, path, d1, d2, 2 * way, 2)
                copies.send(("a2", h, path, which, way, 1), half, half, nearby[axis][way])
        if which == 1:
            gram_end(0)
    factor_inverse(gram_total.at[0], work, inv1)
    for which in range(4):
        for h, path in chunks:
            axis, other = axes[path]
            far = lax.rem(position[axis] + 2, 4)
            d2 = second(position[other], which)
            for way in range(2):
                copies.arrived(
                    ("a2", h, path, which, way, 1), piece(h, path, far, d2, 2 * way, 2), nearby[axis][way]
                )

    product(1, left_all, partial2)

    def for_z(distance):
        return lax.rem(z + 8 + distance, 8)

    def theirs(h, which_core, distance):
        return partial2.at[h, pl.ds(which_core * 64 + for_z(distance) * 8, 8)]

    order = (4, 3, -3, 2, -2, 1, -1, 0)
    for distance in order:
        for h in range(H):
            copies.send(
                ("ps", h, distance), theirs(h, 1 - core, distance), pair_in.at[h, distance + 3], sibling
            )

    def pair_sum(h, distance):
        copies.arrived(("ps", h, distance), pair_in.at[h, distance + 3], sibling)
        mine = partial2[h, pl.ds(core * 64 + for_z(distance) * 8, 8)]
        return mine.astype(F32) + pair_in[h, distance + 3].astype(F32)

    for h in range(H):
        rounded = pair_sum(h, 4).astype(BF16)
        for way in range(2):
            ring_out[h, way, 0, 0:4] = rounded[4 * way : 4 * way + 4]
            copies.send(
                ("rz", h, way, 0),
                ring_out.at[h, way, 0, pl.ds(0, 4)],
                ring_in.at[h, way, 0, pl.ds(0, 4)],
                z_next[way],
            )
    for s in range(1, 4):
        for h in range(H):
            for way in range(2):
                total = pair_sum(h, (4 - s) if way == 0 else (s - 4))
                if s == 1:
                    came = ring_in.at[h, way, 0, pl.ds(0, 4)]
                    copies.arrived(("rz", h, way, 0), came, z_next[way])
                    added = total[4 * way : 4 * way + 4] + came[...].astype(F32)
                    kept = total[4 - 4 * way : 8 - 4 * way]
                    ring_out[h, way, s, 4 * way : 4 * way + 4] = added.astype(BF16)
                    ring_out[h, way, s, 4 - 4 * way : 8 - 4 * way] = kept.astype(BF16)
                else:
                    came = ring_in.at[h, way, s - 1]
                    copies.arrived(("rz", h, way, s - 1), came, z_next[way])
                    ring_out[h, way, s] = (total + came[...].astype(F32)).astype(BF16)
                copies.send(("rz", h, way, s), ring_out.at[h, way, s], ring_in.at[h, way, s], z_next[way])

    def apply(inverse, block):
        return jnp.dot(inverse, block, precision=HIGHEST, preferred_element_type=F32)

    for b in range(8):
        left_out[128 * b : 128 * b + 128, :] = apply(inv1[...], left_y[b].astype(F32)).T.astype(BF16)

    for h in range(H):
        total = pair_sum(h, 0)
        for way in range(2):
            copies.arrived(("rz", h, way, 3), ring_in.at[h, way, 3], z_next[way])
            total = total + ring_in[h, way, 3].astype(F32)
        for b in range(8):
            z_sum[b, PH * h : PH * h + PH, :] = total[b]
    for b in range(8):
        right_y[b] = apply(inv1[...], z_sum[b]).astype(BF16)
    gram_begin(1, right_y)
    gram_middle(1)
    gram_last(1)
    gram_end(1)
    factor_inverse(gram_total.at[1], work, inv2)
    for b in range(8):
        right_out[128 * b : 128 * b + 128, :] = apply(inv2[...], right_y[b].astype(F32)).T.astype(BF16)
    copies.drain()


def slot_order(rows, cols, count):
    slots = rows.shape[0]
    number = jnp.arange(slots, dtype=jnp.int32)
    live = number < count
    group, b = rows // 8, rows % 8
    gx, gy = group // 4, group % 4
    path, blk = b // 4, b % 4
    row_place = path * 64 + jnp.where(path == 0, gx * 16 + gy * 4, gy * 16 + gx * 4) + blk
    key = jnp.where(live[None, :], jnp.stack([rows, cols]), 128)
    inputs = jnp.stack([cols, row_place])
    packed = number[None, :] + 512 * inputs + 65536 * key
    ahead = (key[:, None, :] < key[:, :, None]) | (
        (key[:, None, :] == key[:, :, None]) & (number[None, None, :] < number[None, :, None])
    )
    rank = jnp.sum(ahead.astype(jnp.int32), axis=2)
    hit = rank[:, :, None] == number[None, None, :]
    in_order = jnp.sum(jnp.where(hit, packed[:, :, None], 0), axis=1)
    codes = in_order & 65535
    key_order = in_order >> 16
    keeps = jnp.concatenate(
        [jnp.zeros((2, 1), F32), (key_order[:, 1:] == key_order[:, :-1]).astype(F32)], axis=1
    )
    q = jnp.arange(128, dtype=jnp.int32)
    path, d1, d2, blk = q // 64, q // 16 % 4, q // 4 % 4, q % 4
    left_block = jnp.where(path == 0, d1 * 4 + d2, d2 * 4 + d1) * 8 + path * 4 + blk
    right_block = (2 * (q // 8 % 8) + q // 64) * 8 + q % 8
    block = jnp.stack([left_block, right_block])
    upto = jnp.sum((key[:, :, None] <= block[:, None, :]).astype(jnp.int32), axis=1)
    below = jnp.sum((key[:, :, None] < block[:, None, :]).astype(jnp.int32), axis=1)
    lasts = jnp.where(upto > below, upto - 1, slots)
    return codes.reshape(-1), keeps.reshape(-1), lasts.reshape(-1)


def local(start_panel, block_values, block_rows, block_cols, block_counts):
    slots = block_values.shape[2]
    group_rows, width = start_panel.shape
    nodes_total = group_rows * lax.axis_size("row") * lax.axis_size("col")
    codes, keeps, lasts = slot_order(block_rows[0, 0], block_cols[0, 0], block_counts[0, 0])
    vmem = pl.BlockSpec(memory_space=pltpu.VMEM)
    smem = pl.BlockSpec(memory_space=pltpu.SMEM)
    panel = jax.ShapeDtypeStruct((group_rows, width), BF16)
    tile = pltpu.VMEM((H, 128, PH, 128), BF16)
    return pl.pallas_call(
        functools.partial(kernel, nodes_total),
        out_shape=(panel, panel),
        in_specs=[smem, smem, smem, vmem, pl.BlockSpec(memory_space=pl.ANY)],
        out_specs=(vmem, vmem),
        scratch_shapes=[
            pltpu.VMEM((slots, 128, 128), BF16),
            tile,
            pltpu.VMEM((slots + 1, 128, 128), BF16),
            tile,
            tile,
            pltpu.VMEM((H, 2, 2, 8, PH, 128), BF16),
            pltpu.VMEM((H, 2, 2, 16, PH, 128), BF16),
            pltpu.VMEM((H, 2, 4, 4, PH, 128), BF16),
            pltpu.VMEM((H, 2, 4, 4, PH, 128), F32),
            pltpu.VMEM((H, 2, 2, 2, PH, 128), BF16),
            pltpu.VMEM((H, 2, 2, 4, PH, 128), BF16),
            tile,
            pltpu.VMEM((8, 128, 128), BF16),
            pltpu.VMEM((H, 8, 8, PH, 128), BF16),
            pltpu.VMEM((H, 2, 4, 8, PH, 128), BF16),
            pltpu.VMEM((H, 2, 4, 8, PH, 128), BF16),
            pltpu.VMEM((8, 128, 128), F32),
            pltpu.VMEM((8, 128, 128), BF16),
            pltpu.VMEM((2, 128, 128), F32),
            pltpu.VMEM((2, 16, 8, 128), F32),
            pltpu.VMEM((2, 8, 128), F32),
            pltpu.VMEM((2, 16, 8, 128), F32),
            pltpu.VMEM((2, 128, 128), F32),
            pltpu.VMEM((128, 128), F32),
            pltpu.VMEM((128, 128), F32),
            pltpu.VMEM((128, 128), F32),
            pltpu.SemaphoreType.DMA,
            pltpu.SemaphoreType.DMA((SENDS,)),
            pltpu.SemaphoreType.DMA((SENDS,)),
        ],
        compiler_params=pltpu.CompilerParams(
            collective_id=0, has_side_effects=True, vmem_limit_bytes=60 * 2**20
        ),
        cost_estimate=pl.CostEstimate(
            flops=4 * slots * 128**3, bytes_accessed=2 * slots * 128 * 128, transcendentals=0
        ),
    )(codes, keeps, lasts, start_panel, block_values[0, 0])


def solution(mesh):
    return jax.shard_map(
        local,
        mesh=mesh,
        in_specs=(
            P(("col", "row"), None),
            P("row", "col", None, None, None),
            P("row", "col", None),
            P("row", "col", None),
            P("row", "col"),
        ),
        out_specs=(P(("row", "col"), None), P(("col", "row"), None)),
        check_vma=False,
    )
```

time: 989 us -> 197 us (0.20)
  waiting for transfers between devices: 740 us -> 0 us
  Pallas kernels: 0 us -> 187 us
  local copies, waits for them, and re-layouts: 91.5 us -> 4.68 us
  matrix products: 84 us -> 0 us
  other arithmetic: 48.9 us -> 3.26 us
  between operations: 15.3 us -> 1.33 us
    psum x2 -> x0, waiting for transfers between devices: 486 us -> none  [global_gram(): return lax.psum(partial_value, ('row', 'col'))]
    pallas_call x0 -> x1, Pallas kernels: none -> 187 us  [local(): pl.pallas_call(functools.partial(kernel, nodes_total), out_shape=(panel,...]
    reduce_scatter x2 -> x0, waiting for transfers between devices: 155 us -> none  [the longest x1 87 us: local(): lax.psum_scatter(left_partial, 'col', scatter_dimension=0, tiled=True)]
    all_gather x2 -> x0, waiting for transfers between devices: 98.7 us -> none  [the longest x1 52.5 us: local(): row_tile = lax.all_gather(left_panel, 'col', axis=0, tiled=True)]
    dot_general x8 -> x0, matrix products: 83.4 us -> none  [the longest x2 39.1 us: tile_product(): jnp.einsum('ok,kip->oip', placement, products, precision=lax.Precision.HI...]
    dot_general x4 -> x0, local copies, waits for them, and re-layouts: 63.3 us -> none  [the longest x1 23.6 us: tile_product(): jnp.einsum('kij,kjp->kip', values, selected, preferred_element_type=jnp.f...]
    another operation x10 -> x1, other arithmetic: 45.7 us -> 0.01 us  [slot_order(): block = jnp.stack([left_block, right_block])]
    gather x2 -> x0, local copies, waits for them, and re-layouts: 26.3 us -> none  [tile_product(): selected = jnp.take(pieces, index_in, axis=0)]
  transfers between devices with their start and end apart: 6 -> 0, of which waited for: 6 -> 0; matrix products, arithmetic and copies ran while one was open for 0% -> 0% of each run, Pallas kernels for 0% -> 0%
where the time goes in v1:
time: 197 us
  Pallas kernels  187 us (95%)
  local copies, waits for them, and re-layouts  4.68 us (2%)
  other arithmetic  3.26 us (2%)
    pallas_call x1, Pallas kernels, local(): pl.pallas_call(functools.partial(kernel, nodes_total), out_shape=(panel,...  187 us

profile of v1, /device:TPU:1, one launch (start us, length us, event | category | flops | bytes accessed | tf_op | source)
XLA Modules:
  0.0 196.7 jit_solution(16475829875009485914)
XLA Ops:
  1.3 0.7 fusion.2
  2.1 0.8 add_select_fusion
  2.8 0.2 convert_reduce_fusion.1
  3.0 0.6 fusion.4.lasts
  3.7 0.5 convert_reduce_fusion
  4.1 0.3 select_reduce_fusion
  4.4 0.1 slice_compare_fusion
  4.5 0.1 pad_convert_fusion
  4.6 0.7 reshape.694.keeps
  5.3 0.7 and.309.codes
  5.9 187.4 %shard_map.68 = (bf16[1024,128]{1,0:T(8,128)(2,1)}, bf16[1024,128]{1,0:T(8,128)(2,1)}) custom-call(s32[704]{0:T(1024)} %and.309.codes, f32[704]{0:T(1024)} %reshape.694.keeps, s32[256]{0:T(256)} %fusion.4.lasts, bf16[1024,128]{1,0:T(8,128)(2,1)} %start_ref.1, bf16[352,128,128]{2,1,0:T(8,128)(2,1)} %bitcast.8), custom_call_target="tpu_custom_call" | custom-call | flops 2952790016 | bytes 11534336 | tf_op jit(solution)/shard_map/pallas_call | solution.py:496
  193.4 1.7 copy.10
  195.1 1.7 copy.11
  (5 shorter events, 0.1 us)

commit v2 on v1

v2 whole, which is shorter than its diff:
```python
import functools

import jax
import jax.numpy as jnp
from jax import lax
from jax.experimental import pallas as pl
from jax.experimental.pallas import tpu as pltpu
from jax.sharding import PartitionSpec as P

MESH = pl.DeviceIdType.MESH
F32 = jnp.float32
BF16 = jnp.bfloat16
HIGHEST = lax.Precision.HIGHEST

H = 2
PH = 64
NZ = 8
UNROLL = 16
PARTS = 4
SENDS = 440
GATHER_CUTS = 4
COLUMN_CUTS = 2


class Copies:
    def __init__(self, send_sems, recv_sems):
        self.send_sems, self.recv_sems = send_sems, recv_sems
        self.index, self.sent = {}, []

    def sems(self, name):
        number = self.index.setdefault(name, len(self.index))
        assert number < SENDS
        return self.send_sems.at[number], self.recv_sems.at[number]

    def make(self, name, src, dst, device):
        send, recv = self.sems(name)
        return pltpu.make_async_remote_copy(
            src_ref=src, dst_ref=dst, send_sem=send, recv_sem=recv, device_id=device, device_id_type=MESH
        )

    def send(self, name, src, dst, device):
        copy = self.make(name, src, dst, device)
        copy.start()
        self.sent.append(copy)

    def arrived(self, name, dst, device):
        self.make(name, dst, dst, device).wait_recv()

    def drain(self):
        for copy in self.sent:
            copy.wait_send()
        self.sent = []


def split3(value):
    high = value.astype(BF16).astype(F32)
    rest = value - high
    middle = rest.astype(BF16).astype(F32)
    return high, middle, (rest - middle).astype(BF16).astype(F32)


def factor_begin(gram, work):
    n = gram.shape[0]
    rows = lax.broadcasted_iota(jnp.int32, (n, n), 0)
    cols = lax.broadcasted_iota(jnp.int32, (n, n), 1)
    work[:, :n] = gram
    work[:, n:] = jnp.where(rows == cols, 1.0, 0.0).astype(F32)


def factor_blocks(work, first, last):
    n = work.shape[0]
    lanes = lax.broadcasted_iota(jnp.int32, (16, n), 1)
    subs = lax.broadcasted_iota(jnp.int32, (8, n), 0)

    def block(jb, carry):
        start = pl.multiple_of(jb * 16, 16)
        rows = work[pl.ds(start, 16), :]
        turned = pltpu.roll(rows[:, :n], lax.rem(n - start, n), 1)
        top = [jnp.broadcast_to(turned[:8, i : i + 1], (8, n)) for i in range(16)]
        low = [jnp.broadcast_to(turned[8:, i : i + 1], (8, n)) for i in range(16)]
        rows_top = [rows[:8, :n], rows[:8, n:]]
        rows_low = [rows[8:, :n], rows[8:, n:]]
        scales = [jnp.zeros((8, n), F32), jnp.zeros((8, n), F32)]
        for i in range(16):
            half, sub = i // 8, i % 8
            source, source_rows = (top, rows_top) if half == 0 else (low, rows_low)
            inverse = jnp.broadcast_to(1.0 / source[i][sub : sub + 1, :], (8, n))
            scales[half] = jnp.where(subs == sub, inverse, scales[half])
            pivots = {j: source[j][sub : sub + 1, :] for j in range(i + 1, 16)}
            pivot_rows = [value[sub : sub + 1, :] for value in source_rows]
            if half == 0:
                factor = jnp.where(subs > sub, top[i] * inverse, 0.0)
                for j in range(i + 1, 16):
                    top[j] = top[j] - factor * pivots[j]
                rows_top = [value - factor * pivot for value, pivot in zip(rows_top, pivot_rows)]
                factor = low[i] * inverse
            else:
                factor = jnp.where(subs > sub, low[i] * inverse, 0.0)
            for j in range(i + 1, 16):
                low[j] = low[j] - factor * pivots[j]
            rows_low = [value - factor * pivot for value, pivot in zip(rows_low, pivot_rows)]
        scale = jnp.concatenate(scales, axis=0)
        d = jnp.concatenate([rows_top[0], rows_low[0]], axis=0)
        m = jnp.concatenate([rows_top[1], rows_low[1]], axis=0)
        left = split3(jnp.where(lanes >= start + 16, d * scale, 0.0))
        right = split3(jnp.concatenate([d, m], axis=1))
        pairs = ((0, 0), (0, 1), (1, 0), (1, 1), (0, 2), (2, 0))
        stacked_left = jnp.concatenate([left[a] for a, _ in pairs], axis=0).T.astype(BF16)
        stacked_right = jnp.concatenate([right[b] for _, b in pairs], axis=0).astype(BF16)
        work[...] = work[...] - jnp.dot(stacked_left, stacked_right, preferred_element_type=F32)
        work[pl.ds(start, 16), n:] = m * jnp.sqrt(scale)
        return carry

    lax.fori_loop(first, last, block, 0)


def kernel(
    nodes_total,
    codes,
    keeps,
    lasts,
    start_ref,
    values_hbm,
    left_y,
    right_y,
    inv1,
    inv2,
    values,
    gathered0,
    gathered1,
    sums,
    run_total,
    partial,
    partial2,
    relay1,
    full1,
    mid,
    mid_own,
    full2,
    left_all0,
    left_all1,
    pair_in,
    ring_out,
    ring_in,
    near_sum,
    z_sum,
    gram_part,
    gram_in1,
    gram_slice,
    gram_in2,
    gram_total,
    work,
    local_sem,
    send_sems,
    recv_sems,
):
    gathered, left_all = (gathered0, gathered1), (left_all0, left_all1)
    slots = values_hbm.shape[0]
    r = lax.axis_index("row")
    c = lax.axis_index("col")
    z, core = r // 2, lax.rem(r, 2)
    position = {"x": c // 4, "y": lax.rem(c, 4)}
    x, y = position["x"], position["y"]
    sibling = {"row": 2 * z + 1 - core}
    z_next = ({"row": lax.rem(r + 2, 16)}, {"row": lax.rem(r + 14, 16)})
    nearby = {
        "x": ({"col": lax.rem(c + 4, 16)}, {"col": lax.rem(c + 12, 16)}),
        "y": ({"col": 4 * x + lax.rem(y + 1, 4)}, {"col": 4 * x + lax.rem(y + 3, 4)}),
    }
    along = {
        "x": [{"col": lax.rem(c + 4 * e, 16)} for e in range(4)],
        "y": [{"col": 4 * x + lax.rem(y + e, 4)} for e in range(4)],
    }
    axes = (("x", "y"), ("y", "x"))
    copies = Copies(send_sems, recv_sems)
    paths = range(2)

    load_values = pltpu.make_async_copy(values_hbm, values, local_sem)
    load_values.start()

    barrier = pltpu.get_barrier_semaphore()
    for t in range(1, 16):
        pl.semaphore_signal(barrier, inc=1, device_id={"row": lax.rem(r + t, 16)}, device_id_type=MESH)
        pl.semaphore_signal(barrier, inc=1, device_id={"col": lax.rem(c + t, 16)}, device_id_type=MESH)

    for b in range(8):
        turned = start_ref[128 * b : 128 * b + 128, :].astype(F32).T.astype(BF16)
        for h in range(H):
            gathered[h][r * 8 + b] = turned[PH * h : PH * h + PH, :]
    sums[slots] = jnp.zeros((PH, 128), BF16)
    pl.semaphore_wait(barrier, 30)

    def group(h, number, first=0, count=8):
        return gathered[h].at[pl.ds(number * 8 + first, count)]

    def origin(way, s):
        return lax.rem(r + (32 - 2 * s if way == 0 else 2 * s), 16)

    def origin_sibling(way, s):
        return lax.rem(2 * z + 1 - core + (32 - 2 * s if way == 0 else 2 * s), 16)

    cut = 8 // GATHER_CUTS

    def gather_begin(h):
        for q in range(GATHER_CUTS):
            own = group(h, r, cut * q, cut)
            for way in range(2):
                copies.send(("gz", h, way, 1, q), own, own, z_next[way])
        own = group(h, r)
        copies.send(("gs", h, 0, 0), own, own, sibling)

    def last_cuts(way):
        return range(way * GATHER_CUTS // 2, (way + 1) * GATHER_CUTS // 2)

    def gather_step(h, s):
        for q in range(GATHER_CUTS):
            for way in range(2):
                if s == 4 and q not in last_cuts(way):
                    continue
                part = group(h, origin(way, s), cut * q, cut)
                copies.arrived(("gz", h, way, s, q), part, z_next[way])
                if s < 3 or (s == 3 and q in last_cuts(way)):
                    copies.send(("gz", h, way, s + 1, q), part, part, z_next[way])
        for way in range(2):
            whole = group(h, origin(way, s)) if s < 4 else group(h, origin(way, s), 4 * way, 4)
            copies.send(("gs", h, way, s), whole, whole, sibling)

    def gather_end(h):
        copies.arrived(("gs", h, 0, 0), group(h, 2 * z + 1 - core), sibling)
        for s in range(1, 5):
            for way in range(2):
                number = origin_sibling(way, s)
                piece = group(h, number) if s < 4 else group(h, number, 4 * way, 4)
                copies.arrived(("gs", h, way, s), piece, sibling)

    def product(side, h, part):
        contract = (((1,), (1,)), ((), ())) if side == 0 else (((1,), (0,)), ((), ()))
        panel = gathered[h] if side == 0 else left_all[h]
        steps = slots // UNROLL

        def some_slots(step, total):
            for u in range(UNROLL):
                k = step * UNROLL + u
                code = codes[side * slots + k]
                term = lax.dot_general(panel[code >> 9], values[code & 511], contract, preferred_element_type=F32)
                total = total * keeps[side * slots + k] + term
                sums[k] = total.astype(BF16)
            return total

        total = jnp.zeros((PH, 128), F32) if part == 0 else run_total[...]
        run_total[...] = lax.fori_loop(steps * part // PARTS, steps * (part + 1) // PARTS, some_slots, total)

    def place(side, h):
        out = partial if side == 0 else partial2

        def some_blocks(step, carry):
            for u in range(8):
                q = step * 8 + u
                out[h, q] = sums[lasts[side * 128 + q]]
            return carry

        lax.fori_loop(0, 16, some_blocks, 0)

    def slab(h, path, d1, first=0, count=4):
        return (h, pl.ds(path * 64 + d1 * 16 + first * 4, count * 4))

    def reduce1(h):
        for n in range(2):
            for path in paths:
                axis = axes[path][0]
                far = lax.rem(position[axis] + 2, 4)
                for way in range(2):
                    src = partial.at[slab(h, path, far, 2 * way + n, 1)]
                    dst = relay1.at[h, path, way, pl.ds(4 * n, 4)]
                    copies.send(("r1", h, path, way, n), src, dst, nearby[axis][way])
        for path in paths:
            axis = axes[path][0]
            for way in range(2):
                near = lax.rem(position[axis] + (1 if way == 0 else 3), 4)
                src = partial.at[slab(h, path, near, 2 - 2 * way, 2)]
                dst = full1.at[h, path, way, pl.ds(8 - 8 * way, 8)]
                copies.send(("r1", h, path, way, 2), src, dst, nearby[axis][way])

    def reduce2(h):
        for n in range(2):
            for path in paths:
                axis = axes[path][0]
                for way in range(2):
                    near = lax.rem(position[axis] + (1 if way == 0 else 3), 4)
                    came = relay1.at[h, path, way, pl.ds(4 * n, 4)]
                    copies.arrived(("r1", h, path, way, n), came, nearby[axis][way])
                    where = slab(h, path, near, 2 * way + n, 1)
                    partial[where] = (partial[where].astype(F32) + came[...].astype(F32)).astype(BF16)
                    dst = full1.at[h, path, way, pl.ds(8 * way + 4 * n, 4)]
                    copies.send(("r1", h, path, way, 3 + n), partial.at[where], dst, nearby[axis][way])

    def reduce3(h):
        for path in paths:
            axis, other = axes[path]
            m, m2 = position[axis], position[other]
            for way in range(2):
                came = full1.at[h, path, way]
                copies.arrived(("r1", h, path, way, 2), came.at[pl.ds(8 - 8 * way, 8)], nearby[axis][way])
                for n in range(2):
                    copies.arrived(
                        ("r1", h, path, way, 3 + n), came.at[pl.ds(8 * way + 4 * n, 4)], nearby[axis][way]
                    )
            for e in (2, 1, 3, 0):
                d2 = lax.rem(m2 + e, 4)
                total = partial[slab(h, path, m, d2, 1)].astype(F32)
                for way in range(2):
                    total = total + full1[h, path, way, pl.ds(4 * d2, 4)].astype(F32)
                if e == 0:
                    mid_own[h, path] = total
                else:
                    mid[h, path, e - 1] = total.astype(BF16)
                    copies.send(
                        ("r2", h, path, e), mid.at[h, path, e - 1], full2.at[h, path, e - 1], along[other][e]
                    )

    def piece(h, path, d1, d2, first=0, count=4):
        return left_all[h].at[pl.ds(path * 64 + d1 * 16 + d2 * 4 + first, count)]

    def reduce4(h):
        for path in paths:
            axis, other = axes[path]
            m1, m2 = position[axis], position[other]
            total = mid_own[h, path]
            for e in (1, 3, 2):
                copies.arrived(("r2", h, path, e), full2.at[h, path, e - 1], along[other][e])
                total = total + full2[h, path, e - 1].astype(F32)
            rounded = total.astype(BF16)
            left_all[h][pl.ds(path * 64 + m1 * 16 + m2 * 4, 4)] = rounded
            for b in range(4):
                at = 128 * (path * 4 + b)
                left_y[PH * h : PH * h + PH, at : at + 128] = rounded[b]
            own = piece(h, path, m1, m2)
            for e in (2, 1, 3):
                copies.send(("a1", h, path, e), own, own, along[other][e])
            for way in range(2):
                copies.send(("a2", h, path, 0, way, 0), own, own, nearby[axis][way])

    def gram_begin(tag, panel):
        total = lax.dot_general(panel, panel, (((1,), (1,)), ((), ())), preferred_element_type=F32)
        gram_part[tag] = total * (1.0 / nodes_total)
        gram_in1[tag, r] = gram_part[tag, pl.ds(pl.multiple_of(r * 8, 8), 8), :]
        for t in range(1, 16):
            to = lax.rem(r + t, 16)
            src = gram_part.at[tag, pl.ds(pl.multiple_of(to * 8, 8), 8), :]
            copies.send(("m1", tag, t), src, gram_in1.at[tag, r], {"row": to})

    def gram_middle(tag):
        for t in range(1, 16):
            copies.arrived(("m1", tag, t), gram_in1.at[tag, lax.rem(r + 16 - t, 16)], {"row": lax.rem(r + t, 16)})
        gram_slice[tag] = jnp.sum(gram_in1[tag], axis=0)
        gram_in2[tag, c] = gram_slice[tag]
        for t in range(1, 16):
            copies.send(("m2", tag, t), gram_slice.at[tag], gram_in2.at[tag, c], {"col": lax.rem(c + t, 16)})

    def gram_last(tag):
        for t in range(1, 16):
            copies.arrived(("m2", tag, t), gram_in2.at[tag, lax.rem(c + 16 - t, 16)], {"col": lax.rem(c + t, 16)})
        mine = gram_total.at[tag, pl.ds(pl.multiple_of(r * 8, 8), 8), :]
        mine[...] = jnp.sum(gram_in2[tag], axis=0)
        for t in range(1, 16):
            copies.send(("m3", tag, t), mine, mine, {"row": lax.rem(r + t, 16)})

    def gram_end(tag):
        for t in range(1, 16):
            rows = pl.ds(pl.multiple_of(lax.rem(r + 16 - t, 16) * 8, 8), 8)
            copies.arrived(("m3", tag, t), gram_total.at[tag, rows, :], {"row": lax.rem(r + t, 16)})

    def second(m2, e):
        return lax.rem(m2 + 4 - e, 4)

    def spread1(h):
        for e in (1, 3, 2):
            for path in paths:
                axis, other = axes[path]
                whole = piece(h, path, position[axis], second(position[other], e))
                copies.arrived(("a1", h, path, e), whole, along[other][e])
                for way in range(2):
                    copies.send(("a2", h, path, e, way, 0), whole, whole, nearby[axis][way])

    def spread3(h, which):
        for path in paths:
            axis, other = axes[path]
            m1, m2 = position[axis], position[other]
            d2 = second(m2, which)
            for way in range(2):
                d1 = lax.rem(m1 + (3 if way == 0 else 1), 4)
                copies.arrived(("a2", h, path, which, way, 0), piece(h, path, d1, d2), nearby[axis][way])
                half = piece(h, path, d1, d2, 2 * way, 2)
                copies.send(("a2", h, path, which, way, 1), half, half, nearby[axis][way])

    def spread_end(h):
        for which in (0, 1, 3, 2):
            for path in paths:
                axis, other = axes[path]
                far = lax.rem(position[axis] + 2, 4)
                d2 = second(position[other], which)
                for way in range(2):
                    copies.arrived(
                        ("a2", h, path, which, way, 1), piece(h, path, far, d2, 2 * way, 2), nearby[axis][way]
                    )

    def for_z(distance):
        return lax.rem(z + 8 + distance, 8)

    def column0(h):
        for distance in (4, 3, -3, 2, -2, 1, -1, 0):
            src = partial2.at[h, pl.ds((1 - core) * 64 + for_z(distance) * 8, 8)]
            copies.send(("ps", h, distance), src, pair_in.at[h, distance + 3], sibling)

    def pair_sum(h, distance):
        copies.arrived(("ps", h, distance), pair_in.at[h, distance + 3], sibling)
        mine = partial2[h, pl.ds(core * 64 + for_z(distance) * 8, 8)]
        return mine.astype(F32) + pair_in[h, distance + 3].astype(F32)

    span = 8 // COLUMN_CUTS

    def far_cut(way, q):
        return q // (COLUMN_CUTS // 2) == way

    def column_send(h, way, s, q, total):
        at = pl.ds(span * q, span)
        ring_out[h, way, s, at] = total.astype(BF16)
        copies.send(
            ("rz", h, way, s, q), ring_out.at[h, way, s, at], ring_in.at[h, way, s, at], z_next[way]
        )

    def column1(h):
        total = pair_sum(h, 4)
        for q in range(COLUMN_CUTS):
            for way in range(2):
                if far_cut(way, q):
                    column_send(h, way, 0, q, total[span * q : span * q + span])
        for way in range(2):
            total = pair_sum(h, 3 - 6 * way)
            near_sum[h, way] = total
            for q in range(COLUMN_CUTS):
                if not far_cut(way, q):
                    column_send(h, way, 1, q, total[span * q : span * q + span])

    def column2(h, s):
        if s > 1:
            for way in range(2):
                near_sum[h, way] = pair_sum(h, (4 - s) * (1 - 2 * way))
        for first in (True, False):
            for q in range(COLUMN_CUTS):
                for way in range(2):
                    far = far_cut(way, q)
                    if far == first or (s == 1 and not far):
                        continue
                    at = pl.ds(span * q, span)
                    came = ring_in.at[h, way, s - 1, at]
                    copies.arrived(("rz", h, way, s - 1, q), came, z_next[way])
                    column_send(h, way, s, q, near_sum[h, way, at] + came[...].astype(F32))

    def column3(h):
        total = pair_sum(h, 0)
        for way in range(2):
            for q in range(COLUMN_CUTS):
                came = ring_in.at[h, way, 3, pl.ds(span * q, span)]
                copies.arrived(("rz", h, way, 3, q), came, z_next[way])
            total = total + ring_in[h, way, 3].astype(F32)
        for b in range(8):
            z_sum[PH * h : PH * h + PH, 128 * b : 128 * b + 128] = total[b]

    gather_begin(0)
    gather_step(0, 1)
    gather_begin(1)
    for s in (2, 3):
        gather_step(0, s)
        gather_step(1, s - 1)
    gather_step(0, 4)
    gather_end(0)
    load_values.wait()
    product(0, 0, 0)
    gather_step(1, 3)
    product(0, 0, 1)
    product(0, 0, 2)
    gather_step(1, 4)
    product(0, 0, 3)
    place(0, 0)
    reduce1(0)
    gather_end(1)
    product(0, 1, 0)
    product(0, 1, 1)
    reduce2(0)
    product(0, 1, 2)
    product(0, 1, 3)
    place(0, 1)
    reduce1(1)
    reduce3(0)
    reduce2(1)
    reduce4(0)
    reduce3(1)
    spread1(0)
    spread3(0, 0)
    reduce4(1)
    gram_begin(0, left_y[...])
    spread3(0, 1)
    spread3(0, 3)
    spread3(0, 2)
    spread1(1)
    spread_end(0)
    product(1, 0, 0)
    spread3(1, 0)
    product(1, 0, 1)
    spread3(1, 1)
    spread3(1, 3)
    product(1, 0, 2)
    spread3(1, 2)
    product(1, 0, 3)
    place(1, 0)
    column0(0)
    gram_middle(0)
    column1(0)
    spread_end(1)
    product(1, 1, 0)
    product(1, 1, 1)
    column2(0, 1)
    gram_last(0)
    product(1, 1, 2)
    product(1, 1, 3)
    place(1, 1)
    column0(1)
    column2(0, 2)
    column1(1)
    gram_end(0)
    factor_begin(gram_total[0], work)
    factor_blocks(work, 0, 2)
    column2(0, 3)
    column2(1, 1)
    factor_blocks(work, 2, 4)
    column3(0)
    column2(1, 2)
    factor_blocks(work, 4, 6)
    column2(1, 3)
    factor_blocks(work, 6, 8)
    inv1[...] = work[:, 128:]
    column3(1)
    right_sum = jnp.dot(inv1[...], z_sum[...], precision=HIGHEST, preferred_element_type=F32)
    right_y[...] = right_sum.astype(BF16)
    gram_begin(1, right_y[...])
    gram_middle(1)
    gram_last(1)
    gram_end(1)
    factor_begin(gram_total[1], work)
    factor_blocks(work, 0, 8)
    inv2[...] = work[:, 128:]
    copies.drain()


def apply_kernel(left_y, right_y, inv1, inv2, left_out, right_out):
    for y, inverse, out in ((left_y, inv1, left_out), (right_y, inv2, right_out)):
        parts = split3(inverse[...])
        total = sum(jnp.dot(part.astype(BF16), y[...], preferred_element_type=F32) for part in parts[::-1])
        for b in range(8):
            out[128 * b : 128 * b + 128, :] = total[:, 128 * b : 128 * b + 128].T.astype(BF16)


def slot_order(rows, cols, count):
    slots = rows.shape[0]
    number = jnp.arange(slots, dtype=jnp.int32)
    live = number < count
    group, b = rows // 8, rows % 8
    gx, gy = group // 4, group % 4
    path, blk = b // 4, b % 4
    row_place = path * 64 + jnp.where(path == 0, gx * 16 + gy * 4, gy * 16 + gx * 4) + blk
    key = jnp.where(live[None, :], jnp.stack([rows, cols]), 128)
    inputs = jnp.stack([cols, row_place])
    packed = number[None, :] + 512 * inputs + 65536 * key
    ahead = (key[:, None, :] < key[:, :, None]) | (
        (key[:, None, :] == key[:, :, None]) & (number[None, None, :] < number[None, :, None])
    )
    rank = jnp.sum(ahead.astype(jnp.int32), axis=2)
    hit = rank[:, :, None] == number[None, None, :]
    in_order = jnp.sum(jnp.where(hit, packed[:, :, None], 0), axis=1)
    codes = in_order & 65535
    key_order = in_order >> 16
    keeps = jnp.concatenate(
        [jnp.zeros((2, 1), F32), (key_order[:, 1:] == key_order[:, :-1]).astype(F32)], axis=1
    )
    q = jnp.arange(128, dtype=jnp.int32)
    path, d1, d2, blk = q // 64, q // 16 % 4, q // 4 % 4, q % 4
    left_block = jnp.where(path == 0, d1 * 4 + d2, d2 * 4 + d1) * 8 + path * 4 + blk
    right_block = (2 * (q // 8 % 8) + q // 64) * 8 + q % 8
    block = jnp.stack([left_block, right_block])
    upto = jnp.sum((key[:, :, None] <= block[:, None, :]).astype(jnp.int32), axis=1)
    below = jnp.sum((key[:, :, None] < block[:, None, :]).astype(jnp.int32), axis=1)
    lasts = jnp.where(upto > below, upto - 1, slots)
    return codes.reshape(-1), keeps.reshape(-1), lasts.reshape(-1)


def local(start_panel, block_values, block_rows, block_cols, block_counts):
    slots = block_values.shape[2]
    group_rows, width = start_panel.shape
    nodes_total = group_rows * lax.axis_size("row") * lax.axis_size("col")
    codes, keeps, lasts = slot_order(block_rows[0, 0], block_cols[0, 0], block_counts[0, 0])
    vmem = pl.BlockSpec(memory_space=pltpu.VMEM)
    smem = pl.BlockSpec(memory_space=pltpu.SMEM)
    panel = jax.ShapeDtypeStruct((group_rows, width), BF16)
    tile = pltpu.VMEM((H, 128, PH, 128), BF16)
    half = pltpu.VMEM((128, PH, 128), BF16)
    turned = jax.ShapeDtypeStruct((width, group_rows), BF16)
    square = jax.ShapeDtypeStruct((width, width), F32)
    mixed = pl.pallas_call(
        functools.partial(kernel, nodes_total),
        out_shape=(turned, turned, square, square),
        in_specs=[smem, smem, smem, vmem, pl.BlockSpec(memory_space=pl.ANY)],
        out_specs=(vmem,) * 4,
        scratch_shapes=[
            pltpu.VMEM((slots, 128, 128), BF16),
            half,
            half,
            pltpu.VMEM((slots + 1, PH, 128), BF16),
            pltpu.VMEM((PH, 128), F32),
            tile,
            tile,
            pltpu.VMEM((H, 2, 2, 8, PH, 128), BF16),
            pltpu.VMEM((H, 2, 2, 16, PH, 128), BF16),
            pltpu.VMEM((H, 2, 3, 4, PH, 128), BF16),
            pltpu.VMEM((H, 2, 4, PH, 128), F32),
            pltpu.VMEM((H, 2, 3, 4, PH, 128), BF16),
            half,
            half,
            pltpu.VMEM((H, 8, 8, PH, 128), BF16),
            pltpu.VMEM((H, 2, 4, 8, PH, 128), BF16),
            pltpu.VMEM((H, 2, 4, 8, PH, 128), BF16),
            pltpu.VMEM((H, 2, 8, PH, 128), F32),
            pltpu.VMEM((128, 1024), F32),
            pltpu.VMEM((2, 128, 128), F32),
            pltpu.VMEM((2, 16, 8, 128), F32),
            pltpu.VMEM((2, 8, 128), F32),
            pltpu.VMEM((2, 16, 8, 128), F32),
            pltpu.VMEM((2, 128, 128), F32),
            pltpu.VMEM((128, 256), F32),
            pltpu.SemaphoreType.DMA,
            pltpu.SemaphoreType.DMA((SENDS,)),
            pltpu.SemaphoreType.DMA((SENDS,)),
        ],
        compiler_params=pltpu.CompilerParams(
            collective_id=0, has_side_effects=True, vmem_limit_bytes=60 * 2**20
        ),
        cost_estimate=pl.CostEstimate(
            flops=4 * slots * 128**3, bytes_accessed=2 * slots * 128 * 128, transcendentals=0
        ),
    )(codes, keeps, lasts, start_panel, block_values[0, 0])
    return pl.pallas_call(apply_kernel, out_shape=(panel, panel), in_specs=[vmem] * 4, out_specs=(vmem, vmem))(*mixed)


def solution(mesh):
    return jax.shard_map(
        local,
        mesh=mesh,
        in_specs=(
            P(("col", "row"), None),
            P("row", "col", None, None, None),
            P("row", "col", None),
            P("row", "col", None),
            P("row", "col"),
        ),
        out_specs=(P(("row", "col"), None), P(("col", "row"), None)),
        check_vma=False,
    )
```

time: 197 us -> 158 us (0.80)
  Pallas kernels: 187 us -> 152 us
  local copies, waits for them, and re-layouts: 4.68 us -> 1.34 us
    pallas_call x1 -> x2, Pallas kernels: 187 us -> 152 us  [the longest x1 150 us: local(): pl.pallas_call(functools.partial(kernel, nodes_total), out_shape=(turned,...]
    unnamed x2 -> x0, local copies, waits for them, and re-layouts: 3.34 us -> none
where the time goes in v2:
time: 158 us
  Pallas kernels  152 us (96%)
  other arithmetic  3.2 us (2%)
    pallas_call x1, Pallas kernels, local(): pl.pallas_call(functools.partial(kernel, nodes_total), out_shape=(turned,...  150 us

profile of v2, /device:TPU:1, one launch (start us, length us, event | category | flops | bytes accessed | tf_op | source)
XLA Modules:
  0.0 158.3 jit_solution(6504176288684892275)
XLA Ops:
  1.3 0.7 fusion.2
  2.1 0.8 add_select_fusion
  2.8 0.2 convert_reduce_fusion.1
  3.0 0.5 fusion.4.lasts
  3.6 0.5 convert_reduce_fusion
  4.1 0.3 select_reduce_fusion
  4.4 0.1 slice_compare_fusion
  4.4 0.1 pad_convert_fusion
  4.5 0.7 reshape.694.keeps
  5.2 0.7 and.309.codes
  5.9 150.0 %shard_map.68 = (bf16[128,1024]{1,0:T(8,128)(2,1)}, bf16[128,1024]{1,0:T(8,128)(2,1)}, f32[128,128]{1,0:T(8,128)}, f32[128,128]{1,0:T(8,128)}) custom-call(s32[704]{0:T(1024)} %and.309.codes, f32[704]{0:T(1024)} %reshape.694.keeps, s32[256]{0:T(256)} %fusion.4.lasts, bf16[1024,128]{1,0:T(8,128)(2,1)} %start_ref.1, bf16[352,128,128]{2,1,0:T(8,128)(2,1)} %bitcast.8), custom_call_target="tpu_custom_call" | custom-call | flops 2952790016 | bytes 11534336 | tf_op jit(solution)/shard_map/pallas_call | solution.py:609
  155.9 2.4 %shard_map.69 = (bf16[1024,128]{1,0:T(8,128)(2,1)}, bf16[1024,128]{1,0:T(8,128)(2,1)}) custom-call(bf16[128,1024]{1,0:T(8,128)(2,1)} %get-tuple-element.6.left_y, bf16[128,1024]{1,0:T(8,128)(2,1)} %get-tuple-element.7.right_y, f32[128,128]{1,0:T(8,128)} %get-tuple-element.8.inv1, f32[128,128]{1,0:T(8,128)} %get-tuple-element.9.inv2), custom_call_target="tpu_custom_call" | custom-call | tf_op jit(solution)/shard_map/pallas_call | solution.py:651
  (5 shorter events, 0.1 us)

commit v3 on v2

--- a/solution.py
+++ b/solution.py
@@ -14,10 +14,10 @@
 
 H = 2
 PH = 64
-NZ = 8
 UNROLL = 16
 PARTS = 4
-SENDS = 440
+SENDS = 64
+ARRIVALS = 172
 GATHER_CUTS = 4
 COLUMN_CUTS = 2
 
@@ -25,26 +25,37 @@
 class Copies:
     def __init__(self, send_sems, recv_sems):
         self.send_sems, self.recv_sems = send_sems, recv_sems
-        self.index, self.sent = {}, []
-
-    def sems(self, name):
+        self.index, self.sent, self.count = {}, [], 0
+
+    def arrival(self, name):
         number = self.index.setdefault(name, len(self.index))
-        assert number < SENDS
-        return self.send_sems.at[number], self.recv_sems.at[number]
-
-    def make(self, name, src, dst, device):
-        send, recv = self.sems(name)
-        return pltpu.make_async_remote_copy(
-            src_ref=src, dst_ref=dst, send_sem=send, recv_sem=recv, device_id=device, device_id_type=MESH
+        assert number < ARRIVALS, number
+        return self.recv_sems.at[number]
+
+    def send(self, name, src, dst, device):
+        if len(self.sent) == SENDS:
+            self.sent.pop(0).wait_send()
+        copy = pltpu.make_async_remote_copy(
+            src_ref=src,
+            dst_ref=dst,
+            send_sem=self.send_sems.at[self.count % SENDS],
+            recv_sem=self.arrival(name),
+            device_id=device,
+            device_id_type=MESH,
         )
-
-    def send(self, name, src, dst, device):
-        copy = self.make(name, src, dst, device)
+        self.count += 1
         copy.start()
         self.sent.append(copy)
 
     def arrived(self, name, dst, device):
-        self.make(name, dst, dst, device).wait_recv()
+        pltpu.make_async_remote_copy(
+            src_ref=dst,
+            dst_ref=dst,
+            send_sem=self.send_sems.at[0],
+            recv_sem=self.arrival(name),
+            device_id=device,
+            device_id_type=MESH,
+        ).wait_recv()
 
     def drain(self):
         for copy in self.sent:
@@ -196,9 +207,6 @@
     def origin(way, s):
         return lax.rem(r + (32 - 2 * s if way == 0 else 2 * s), 16)
 
-    def origin_sibling(way, s):
-        return lax.rem(2 * z + 1 - core + (32 - 2 * s if way == 0 else 2 * s), 16)
-
     cut = 8 // GATHER_CUTS
 
     def gather_begin(h):
@@ -207,7 +215,7 @@
             for way in range(2):
                 copies.send(("gz", h, way, 1, q), own, own, z_next[way])
         own = group(h, r)
-        copies.send(("gs", h, 0, 0), own, own, sibling)
+        copies.send(("gs", h), own, own, sibling)
 
     def last_cuts(way):
         return range(way * GATHER_CUTS // 2, (way + 1) * GATHER_CUTS // 2)
@@ -223,15 +231,10 @@
                     copies.send(("gz", h, way, s + 1, q), part, part, z_next[way])
         for way in range(2):
             whole = group(h, origin(way, s)) if s < 4 else group(h, origin(way, s), 4 * way, 4)
-            copies.send(("gs", h, way, s), whole, whole, sibling)
+            copies.send(("gs", h), whole, whole, sibling)
 
     def gather_end(h):
-        copies.arrived(("gs", h, 0, 0), group(h, 2 * z + 1 - core), sibling)
-        for s in range(1, 5):
-            for way in range(2):
-                number = origin_sibling(way, s)
-                piece = group(h, number) if s < 4 else group(h, number, 4 * way, 4)
-                copies.arrived(("gs", h, way, s), piece, sibling)
+        copies.arrived(("gs", h), gathered[h].at[pl.ds(0, 64)], sibling)
 
     def product(side, h, part):
         contract = (((1,), (1,)), ((), ())) if side == 0 else (((1,), (0,)), ((), ()))
@@ -279,7 +282,7 @@
                 near = lax.rem(position[axis] + (1 if way == 0 else 3), 4)
                 src = partial.at[slab(h, path, near, 2 - 2 * way, 2)]
                 dst = full1.at[h, path, way, pl.ds(8 - 8 * way, 8)]
-                copies.send(("r1", h, path, way, 2), src, dst, nearby[axis][way])
+                copies.send(("r1", h, path), src, dst, nearby[axis][way])
 
     def reduce2(h):
         for n in range(2):
@@ -292,19 +295,13 @@
                     where = slab(h, path, near, 2 * way + n, 1)
                     partial[where] = (partial[where].astype(F32) + came[...].astype(F32)).astype(BF16)
                     dst = full1.at[h, path, way, pl.ds(8 * way + 4 * n, 4)]
-                    copies.send(("r1", h, path, way, 3 + n), partial.at[where], dst, nearby[axis][way])
+                    copies.send(("r1", h, path), partial.at[where], dst, nearby[axis][way])
 
     def reduce3(h):
         for path in paths:
             axis, other = axes[path]
             m, m2 = position[axis], position[other]
-            for way in range(2):
-                came = full1.at[h, path, way]
-                copies.arrived(("r1", h, path, way, 2), came.at[pl.ds(8 - 8 * way, 8)], nearby[axis][way])
-                for n in range(2):
-                    copies.arrived(
-                        ("r1", h, path, way, 3 + n), came.at[pl.ds(8 * way + 4 * n, 4)], nearby[axis][way]
-                    )
+            copies.arrived(("r1", h, path), full1.at[h, path], nearby[axis][0])
             for e in (2, 1, 3, 0):
                 d2 = lax.rem(m2 + e, 4)
                 total = partial[slab(h, path, m, d2, 1)].astype(F32)
@@ -315,7 +312,7 @@
                 else:
                     mid[h, path, e - 1] = total.astype(BF16)
                     copies.send(
-                        ("r2", h, path, e), mid.at[h, path, e - 1], full2.at[h, path, e - 1], along[other][e]
+                        ("r2", h, path), mid.at[h, path, e - 1], full2.at[h, path, e - 1], along[other][e]
                     )
 
     def piece(h, path, d1, d2, first=0, count=4):
@@ -326,8 +323,8 @@
             axis, other = axes[path]
             m1, m2 = position[axis], position[other]
             total = mid_own[h, path]
+            copies.arrived(("r2", h, path), full2.at[h, path], along[other][1])
             for e in (1, 3, 2):
-                copies.arrived(("r2", h, path, e), full2.at[h, path, e - 1], along[other][e])
                 total = total + full2[h, path, e - 1].astype(F32)
             rounded = total.astype(BF16)
             left_all[h][pl.ds(path * 64 + m1 * 16 + m2 * 4, 4)] = rounded
@@ -347,28 +344,24 @@
         for t in range(1, 16):
             to = lax.rem(r + t, 16)
             src = gram_part.at[tag, pl.ds(pl.multiple_of(to * 8, 8), 8), :]
-            copies.send(("m1", tag, t), src, gram_in1.at[tag, r], {"row": to})
+            copies.send(("m1", tag), src, gram_in1.at[tag, r], {"row": to})
 
     def gram_middle(tag):
-        for t in range(1, 16):
-            copies.arrived(("m1", tag, t), gram_in1.at[tag, lax.rem(r + 16 - t, 16)], {"row": lax.rem(r + t, 16)})
+        copies.arrived(("m1", tag), gram_in1.at[tag, pl.ds(0, 15)], sibling)
         gram_slice[tag] = jnp.sum(gram_in1[tag], axis=0)
         gram_in2[tag, c] = gram_slice[tag]
         for t in range(1, 16):
-            copies.send(("m2", tag, t), gram_slice.at[tag], gram_in2.at[tag, c], {"col": lax.rem(c + t, 16)})
+            copies.send(("m2", tag), gram_slice.at[tag], gram_in2.at[tag, c], {"col": lax.rem(c + t, 16)})
 
     def gram_last(tag):
-        for t in range(1, 16):
-            copies.arrived(("m2", tag, t), gram_in2.at[tag, lax.rem(c + 16 - t, 16)], {"col": lax.rem(c + t, 16)})
+        copies.arrived(("m2", tag), gram_in2.at[tag, pl.ds(0, 15)], nearby["x"][0])
         mine = gram_total.at[tag, pl.ds(pl.multiple_of(r * 8, 8), 8), :]
         mine[...] = jnp.sum(gram_in2[tag], axis=0)
         for t in range(1, 16):
-            copies.send(("m3", tag, t), mine, mine, {"row": lax.rem(r + t, 16)})
+            copies.send(("m3", tag), mine, mine, {"row": lax.rem(r + t, 16)})
 
     def gram_end(tag):
-        for t in range(1, 16):
-            rows = pl.ds(pl.multiple_of(lax.rem(r + 16 - t, 16) * 8, 8), 8)
-            copies.arrived(("m3", tag, t), gram_total.at[tag, rows, :], {"row": lax.rem(r + t, 16)})
+        copies.arrived(("m3", tag), gram_total.at[tag, pl.ds(0, 120), :], sibling)
 
     def second(m2, e):
         return lax.rem(m2 + 4 - e, 4)
@@ -391,18 +384,10 @@
                 d1 = lax.rem(m1 + (3 if way == 0 else 1), 4)
                 copies.arrived(("a2", h, path, which, way, 0), piece(h, path, d1, d2), nearby[axis][way])
                 half = piece(h, path, d1, d2, 2 * way, 2)
-                copies.send(("a2", h, path, which, way, 1), half, half, nearby[axis][way])
+                copies.send(("a3", h), half, half, nearby[axis][way])
 
     def spread_end(h):
-        for which in (0, 1, 3, 2):
-            for path in paths:
-                axis, other = axes[path]
-                far = lax.rem(position[axis] + 2, 4)
-                d2 = second(position[other], which)
-                for way in range(2):
-                    copies.arrived(
-                        ("a2", h, path, which, way, 1), piece(h, path, far, d2, 2 * way, 2), nearby[axis][way]
-                    )
+        copies.arrived(("a3", h), left_all[h].at[pl.ds(0, 32)], nearby["x"][0])
 
     def for_z(distance):
         return lax.rem(z + 8 + distance, 8)
@@ -425,8 +410,9 @@
     def column_send(h, way, s, q, total):
         at = pl.ds(span * q, span)
         ring_out[h, way, s, at] = total.astype(BF16)
+        name = ("rz", h, way, s, q) if s < 3 else ("rz", h)
         copies.send(
-            ("rz", h, way, s, q), ring_out.at[h, way, s, at], ring_in.at[h, way, s, at], z_next[way]
+            name, ring_out.at[h, way, s, at], ring_in.at[h, way, s, at], z_next[way]
         )
 
     def column1(h):
@@ -459,10 +445,8 @@
 
     def column3(h):
         total = pair_sum(h, 0)
+        copies.arrived(("rz", h), ring_in.at[h, 0, pl.ds(0, 2)], z_next[0])
         for way in range(2):
-            for q in range(COLUMN_CUTS):
-                came = ring_in.at[h, way, 3, pl.ds(span * q, span)]
-                copies.arrived(("rz", h, way, 3, q), came, z_next[way])
             total = total + ring_in[h, way, 3].astype(F32)
         for b in range(8):
             z_sum[PH * h : PH * h + PH, 128 * b : 128 * b + 128] = total[b]
@@ -639,7 +623,7 @@
             pltpu.VMEM((128, 256), F32),
             pltpu.SemaphoreType.DMA,
             pltpu.SemaphoreType.DMA((SENDS,)),
-            pltpu.SemaphoreType.DMA((SENDS,)),
+            pltpu.SemaphoreType.DMA((ARRIVALS,)),
         ],
         compiler_params=pltpu.CompilerParams(
             collective_id=0, has_side_effects=True, vmem_limit_bytes=60 * 2**20

time: 158 us -> 152 us (0.962)
  Pallas kernels: 152 us -> 146 us
    pallas_call x1, Pallas kernels: 150 us -> 144 us  [local(): pl.pallas_call(functools.partial(kernel, nodes_total), out_shape=(turned,...]
where the time goes in v3:
time: 152 us
  Pallas kernels  146 us (96%)
  other arithmetic  3.2 us (2%)
    pallas_call x1, Pallas kernels, local(): pl.pallas_call(functools.partial(kernel, nodes_total), out_shape=(turned,...  144 us

profile of v3, /device:TPU:1, one launch (start us, length us, event | category | flops | bytes accessed | tf_op | source)
XLA Modules:
  0.0 152.0 jit_solution(12275918054436900138)
XLA Ops:
  1.3 0.7 fusion.2
  2.1 0.8 add_select_fusion
  2.8 0.2 convert_reduce_fusion.1
  3.0 0.5 fusion.4.lasts
  3.6 0.5 convert_reduce_fusion
  4.1 0.3 select_reduce_fusion
  4.4 0.1 slice_compare_fusion
  4.4 0.1 pad_convert_fusion
  4.5 0.7 reshape.694.keeps
  5.2 0.7 and.309.codes
  5.9 143.8 %shard_map.68 = (bf16[128,1024]{1,0:T(8,128)(2,1)}, bf16[128,1024]{1,0:T(8,128)(2,1)}, f32[128,128]{1,0:T(8,128)}, f32[128,128]{1,0:T(8,128)}) custom-call(s32[704]{0:T(1024)} %and.309.codes, f32[704]{0:T(1024)} %reshape.694.keeps, s32[256]{0:T(256)} %fusion.4.lasts, bf16[1024,128]{1,0:T(8,128)(2,1)} %start_ref.1, bf16[352,128,128]{2,1,0:T(8,128)(2,1)} %bitcast.8), custom_call_target="tpu_custom_call" | custom-call | flops 2952790016 | bytes 11534336 | tf_op jit(solution)/shard_map/pallas_call | solution.py:593
  149.7 2.4 %shard_map.69 = (bf16[1024,128]{1,0:T(8,128)(2,1)}, bf16[1024,128]{1,0:T(8,128)(2,1)}) custom-call(bf16[128,1024]{1,0:T(8,128)(2,1)} %get-tuple-element.6.left_y, bf16[128,1024]{1,0:T(8,128)(2,1)} %get-tuple-element.7.right_y, f32[128,128]{1,0:T(8,128)} %get-tuple-element.8.inv1, f32[128,128]{1,0:T(8,128)} %get-tuple-element.9.inv2), custom_call_target="tpu_custom_call" | custom-call | tf_op jit(solution)/shard_map/pallas_call | solution.py:635
  (5 shorter events, 0.1 us)

commit v4 on v3

--- a/solution.py
+++ b/solution.py
@@ -14,7 +14,7 @@
 
 H = 2
 PH = 64
-UNROLL = 16
+UNROLL = 32
 PARTS = 4
 SENDS = 64
 ARRIVALS = 172

time: 152 us -> 151 us (level)
    pallas_call x1, Pallas kernels: 144 us -> 142 us  [local(): pl.pallas_call(functools.partial(kernel, nodes_total), out_shape=(turned,...]
where the time goes in v4:
time: 151 us; the launch traced here: 150 us
  Pallas kernels  145 us (96%)
  other arithmetic  3.2 us (2%)
    pallas_call x1, Pallas kernels, local(): pl.pallas_call(functools.partial(kernel, nodes_total), out_shape=(turned,...  142 us

profile of v4, /device:TPU:1, one launch (start us, length us, event | category | flops | bytes accessed | tf_op | source)
XLA Modules:
  0.0 150.5 jit_solution(1879079658459038561)
XLA Ops:
  1.3 0.7 fusion.2
  2.1 0.8 add_select_fusion
  2.8 0.2 convert_reduce_fusion.1
  3.0 0.5 fusion.4.lasts
  3.6 0.5 convert_reduce_fusion
  4.1 0.3 select_reduce_fusion
  4.4 0.1 slice_compare_fusion
  4.4 0.1 pad_convert_fusion
  4.5 0.7 reshape.694.keeps
  5.2 0.7 and.309.codes
  5.9 142.2 %shard_map.68 = (bf16[128,1024]{1,0:T(8,128)(2,1)}, bf16[128,1024]{1,0:T(8,128)(2,1)}, f32[128,128]{1,0:T(8,128)}, f32[128,128]{1,0:T(8,128)}) custom-call(s32[704]{0:T(1024)} %and.309.codes, f32[704]{0:T(1024)} %reshape.694.keeps, s32[256]{0:T(256)} %fusion.4.lasts, bf16[1024,128]{1,0:T(8,128)(2,1)} %start_ref.1, bf16[352,128,128]{2,1,0:T(8,128)(2,1)} %bitcast.8), custom_call_target="tpu_custom_call" | custom-call | flops 2952790016 | bytes 11534336 | tf_op jit(solution)/shard_map/pallas_call | solution.py:593
  148.1 2.4 %shard_map.69 = (bf16[1024,128]{1,0:T(8,128)(2,1)}, bf16[1024,128]{1,0:T(8,128)(2,1)}) custom-call(bf16[128,1024]{1,0:T(8,128)(2,1)} %get-tuple-element.6.left_y, bf16[128,1024]{1,0:T(8,128)(2,1)} %get-tuple-element.7.right_y, f32[128,128]{1,0:T(8,128)} %get-tuple-element.8.inv1, f32[128,128]{1,0:T(8,128)} %get-tuple-element.9.inv2), custom_call_target="tpu_custom_call" | custom-call | tf_op jit(solution)/shard_map/pallas_call | solution.py:635
  (5 shorter events, 0.1 us)

commit v5 on v4

--- a/solution.py
+++ b/solution.py
@@ -14,7 +14,7 @@
 
 H = 2
 PH = 64
-UNROLL = 32
+UNROLL = 44
 PARTS = 4
 SENDS = 64
 ARRIVALS = 172

time: 151 us -> 148 us (0.980)
  Pallas kernels: 145 us -> 142 us
    pallas_call x1, Pallas kernels: 142 us -> 140 us  [local(): pl.pallas_call(functools.partial(kernel, nodes_total), out_shape=(turned,...]
where the time goes in v5:
time: 148 us
  Pallas kernels  142 us (96%)
  other arithmetic  3.2 us (2%)
    pallas_call x1, Pallas kernels, local(): pl.pallas_call(functools.partial(kernel, nodes_total), out_shape=(turned,...  140 us

profile of v5, /device:TPU:1, one launch (start us, length us, event | category | flops | bytes accessed | tf_op | source)
XLA Modules:
  0.0 148.1 jit_solution(2859754137841923660)
XLA Ops:
  1.3 0.7 fusion.2
  2.1 0.8 add_select_fusion
  2.8 0.2 convert_reduce_fusion.1
  3.0 0.5 fusion.4.lasts
  3.6 0.5 convert_reduce_fusion
  4.1 0.3 select_reduce_fusion
  4.4 0.1 slice_compare_fusion
  4.4 0.1 pad_convert_fusion
  4.5 0.7 reshape.694.keeps
  5.2 0.7 and.309.codes
  5.9 139.8 %shard_map.68 = (bf16[128,1024]{1,0:T(8,128)(2,1)}, bf16[128,1024]{1,0:T(8,128)(2,1)}, f32[128,128]{1,0:T(8,128)}, f32[128,128]{1,0:T(8,128)}) custom-call(s32[704]{0:T(1024)} %and.309.codes, f32[704]{0:T(1024)} %reshape.694.keeps, s32[256]{0:T(256)} %fusion.4.lasts, bf16[1024,128]{1,0:T(8,128)(2,1)} %start_ref.1, bf16[352,128,128]{2,1,0:T(8,128)(2,1)} %bitcast.8), custom_call_target="tpu_custom_call" | custom-call | flops 2952790016 | bytes 11534336 | tf_op jit(solution)/shard_map/pallas_call | solution.py:593
  145.7 2.4 %shard_map.69 = (bf16[1024,128]{1,0:T(8,128)(2,1)}, bf16[1024,128]{1,0:T(8,128)(2,1)}) custom-call(bf16[128,1024]{1,0:T(8,128)(2,1)} %get-tuple-element.6.left_y, bf16[128,1024]{1,0:T(8,128)(2,1)} %get-tuple-element.7.right_y, f32[128,128]{1,0:T(8,128)} %get-tuple-element.8.inv1, f32[128,128]{1,0:T(8,128)} %get-tuple-element.9.inv2), custom_call_target="tpu_custom_call" | custom-call | tf_op jit(solution)/shard_map/pallas_call | solution.py:635
  (5 shorter events, 0.1 us)
